TPU v7x, 32 devices: a whole 2x2x4 slice. The times are simulated.
32 devices in a mesh: groups: 2 (over y), row: 2 (over x), col: 4 (over z), depth: 2 (over core).
Axes of the slice: x: 2, y: 2, z: 4, core: 2. Of those that a mesh axis runs over, the one named last changes fastest.
Arguments:
- layer_input: bfloat16 [4, 224, 4096], P(('groups', 'depth'), 'row', 'col'), parts along dimension 0, may hold values from -6 to 6
- out_grad: bfloat16 [4, 224, 4096], P(('groups', 'depth'), 'row', 'col'), parts along dimension 0, may hold values from -6 to 6
- gate_pre: bfloat16 [4, 224, 14336], P(('groups', 'depth'), 'col', 'row'), parts along dimension 0, may hold values from -6 to 6
- up_pre: bfloat16 [4, 224, 14336], P(('groups', 'depth'), 'col', 'row'), parts along dimension 0, may hold values from -6 to 6
- gate_weight: bfloat16 [4096, 14336], P('col', ('row', 'depth')), may hold values from -0.09375 to 0.09375
- up_weight: bfloat16 [4096, 14336], P('col', ('row', 'depth')), may hold values from -0.09375 to 0.09375
- down_weight: bfloat16 [14336, 4096], P(('row', 'depth'), 'col'), may hold values from -0.046875 to 0.046875
Outputs:
- input_grad: bfloat16 [4, 224, 4096], P(('groups', 'depth'), 'row', 'col'), parts along dimension 0
- gate_weight_grad: bfloat16 [4, 4096, 14336], P(('groups', 'depth'), 'col', 'row'), parts along dimension 0
- up_weight_grad: bfloat16 [4, 4096, 14336], P(('groups', 'depth'), 'col', 'row'), parts along dimension 0
- down_weight_grad: bfloat16 [4, 14336, 4096], P(('groups', 'depth'), 'row', 'col'), parts along dimension 0
There are 2 independent parts, one for each index of `groups`. A program takes and returns all parts, laid end to end along the dimension named above; an argument that names none is the same for every part. Nothing has to cross between parts.
All inputs are finite; a program needn't handle non-finite values.
Results may differ from a plain program's by a relative error of at most 0.03.
Values may be sent and summed in bfloat16 or wider, within the bound.
A program may use at most 192 MiB of HBM per device.

v0:
```python
import jax
import jax.numpy as jnp
from jax import lax
from jax.sharding import PartitionSpec as P


def swiglu_grads(hidden_grad, gate_rows, up_rows):
    gate_value = gate_rows.astype(jnp.float32)
    up_value = up_rows.astype(jnp.float32)
    sig = jax.nn.sigmoid(gate_value)
    silu_value = gate_value * sig
    hidden = (silu_value * up_value).astype(jnp.bfloat16)
    gate_grad = (hidden_grad * up_value * sig * (1.0 + gate_value * (1.0 - sig))).astype(
        jnp.bfloat16
    )
    up_grad = (hidden_grad * silu_value).astype(jnp.bfloat16)
    return (gate_grad, up_grad, hidden)


def times_transposed(left, right):
    return lax.dot_general(
        left, right, (((1,), (1,)), ((), ())), preferred_element_type=jnp.float32
    )


def over_tokens(left, right):
    return lax.dot_general(
        left, right, (((0,), (0,)), ((), ())), preferred_element_type=jnp.float32
    )


def shards(layer_input, out_grad, gate_pre, up_pre, gate_weight, up_weight, down_weight):
    gate_full, up_full, down_full = (
        lax.all_gather(gate_weight, "depth", axis=1, tiled=True),
        lax.all_gather(up_weight, "depth", axis=1, tiled=True),
        lax.all_gather(down_weight, "depth", axis=0, tiled=True),
    )
    input_rows, grad_rows = (
        lax.all_gather(layer_input[0], "row", axis=0, tiled=True),
        lax.all_gather(out_grad[0], "row", axis=0, tiled=True),
    )
    gate_rows, up_rows = (
        lax.all_gather(gate_pre[0], "col", axis=0, tiled=True),
        lax.all_gather(up_pre[0], "col", axis=0, tiled=True),
    )
    partial_hidden = times_transposed(grad_rows, down_full)
    hidden_grad = lax.psum(partial_hidden.astype(jnp.bfloat16), "col").astype(jnp.float32)
    gate_grad, up_grad, hidden = swiglu_grads(hidden_grad, gate_rows, up_rows)
    gate_wgrad = over_tokens(input_rows, gate_grad).astype(jnp.bfloat16)
    up_wgrad = over_tokens(input_rows, up_grad).astype(jnp.bfloat16)
    down_wgrad = over_tokens(hidden, grad_rows).astype(jnp.bfloat16)
    input_share = lax.psum_scatter(
        (times_transposed(gate_grad, gate_full) + times_transposed(up_grad, up_full)).astype(
            jnp.bfloat16
        ),
        "row",
        scatter_dimension=0,
        tiled=True,
    )
    return (input_share[None], gate_wgrad[None], up_wgrad[None], down_wgrad[None])


def solution(mesh):
    return jax.shard_map(
        shards,
        mesh=mesh,
        in_specs=(
            P(("groups", "depth"), "row", "col"),
            P(("groups", "depth"), "row", "col"),
            P(("groups", "depth"), "col", "row"),
            P(("groups", "depth"), "col", "row"),
            P("col", ("row", "depth")),
            P("col", ("row", "depth")),
            P(("row", "depth"), "col"),
        ),
        out_specs=(
            P(("groups", "depth"), "row", "col"),
            P(("groups", "depth"), "col", "row"),
            P(("groups", "depth"), "col", "row"),
            P(("groups", "depth"), "row", "col"),
        ),
        check_vma=False,
    )
```

profile of v0, /device:TPU:0, one launch (start us, length us, event | category | flops | bytes accessed | tf_op | source)
XLA Modules:
  0.0 433.5 jit_solution(16787232423276558372)
XLA Ops:
  7.2 0.0 copy-start.1
  7.2 0.0 all-gather.10.cloned.1.call-start
  7.2 0.7 all-gather.10.cloned.1.call-update
  7.9 0.0 all-gather.18.cloned.1.call-start
  8.0 0.7 all-gather.18.cloned.1.call-update
  8.7 0.0 all-gather.16.cloned.1.call-start
  8.7 0.7 all-gather.16.cloned.1.call-update
  9.4 0.0 all-reduce.2.cloned.1.call-start
  9.4 0.0 copy-done.1
  9.4 9.2 %all-gather = bf16[1,224,1024]{2,1,0:T(8,128)(2,1)S(1)} all-gather(bf16[1,112,1024]{2,1,0:T(8,128)(2,1)S(1)} %copy-done.1), channel_id=2, replica_groups=mesh['groups'=2,'row'=2,'col'=4,'depth'=2] {'row'}, dimensions={1}, use_global_device_ids=true | all-gather | bytes 688128 | tf_op jit(solution)/shard_map/all_gather | solution.py:40
  18.7 20.7 %all-gather.10.cloned.1.call-done = bf16[7168,1024]{1,0:T(8,128)(2,1)} async-done(((bf16[3584,1024]{1,0:T(8,128)(2,1)}), bf16[7168,1024]{1,0:T(8,128)(2,1)}) %all-gather.10.cloned.1.call-update) | async-done | bytes 14680080 | tf_op jit(solution)/shard_map/all_gather | solution.py:36
  39.3 15.9 %convolution_convert_fusion = bf16[224,7168]{1,0:T(8,128)(2,1)} fusion(bf16[7168,1024]{1,0:T(8,128)(2,1)} %all-gather.10.cloned.1.call-done, bf16[1,224,1024]{2,1,0:T(8,128)(2,1)S(1)} %all-gather), kind=kOutput, calls=%fused_computation.6 | convolution fusion | flops 3289939968 | bytes 18350080 | tf_op jit(solution)/shard_map/dot_general | solution.py:21
  55.3 0.0 all-reduce.2.cloned.1.call-update
  55.3 0.0 copy-start.2
  55.3 0.0 all-gather.12.cloned.1.call-start
  55.4 0.5 all-gather.12.cloned.1.call-update
  55.9 0.0 all-gather.14.cloned.1.call-start
  56.0 0.5 all-gather.14.cloned.1.call-update
  56.5 0.0 reduce-scatter.2.cloned.1.call-start
  56.5 0.0 copy-done.2
  56.5 8.7 %all-gather.3 = bf16[1,224,1024]{2,1,0:T(8,128)(2,1)} all-gather(bf16[1,112,1024]{2,1,0:T(8,128)(2,1)S(1)} %copy-done.2), channel_id=5, replica_groups=mesh['groups'=2,'row'=2,'col'=4,'depth'=2] {'row'}, dimensions={1}, use_global_device_ids=true | all-gather | bytes 688128 | tf_op jit(solution)/shard_map/all_gather | solution.py:39
  65.3 41.4 %all-gather.18.cloned.1.call-done = bf16[1,224,7168]{2,1,0:T(8,128)(2,1)} async-done(((bf16[1,56,7168]{2,1,0:T(8,128)(2,1)}), bf16[1,224,7168]{2,1,0:T(8,128)(2,1)}) %all-gather.18.cloned.1.call-update) | async-done | bytes 3211280 | tf_op jit(solution)/shard_map/all_gather | solution.py:43
  106.7 64.8 %all-gather.16.cloned.1.call-done = bf16[1,224,7168]{2,1,0:T(8,128)(2,1)} async-done(((bf16[1,56,7168]{2,1,0:T(8,128)(2,1)}), bf16[1,224,7168]{2,1,0:T(8,128)(2,1)}) %all-gather.16.cloned.1.call-update) | async-done | bytes 3211280 | tf_op jit(solution)/shard_map/all_gather | solution.py:44
  171.5 10.8 %convert_bitcast_fusion = bf16[1,7168,1024]{2,1,0:T(8,128)(2,1)} fusion(bf16[1,224,7168]{2,1,0:T(8,128)(2,1)} %all-gather.16.cloned.1.call-done, bf16[1,224,7168]{2,1,0:T(8,128)(2,1)} %all-gather.18.cloned.1.call-done, bf16[1,224,1024]{2,1,0:T(8,128)(2,1)S(1)} %all-gather), kind=kOutput, calls=%fused_computation | convolution fusion | flops 3308519424 | bytes 21561344 | tf_op jit(solution)/shard_map/dot_general | solution.py:27
  182.3 113.9 %all-reduce.2.cloned.1.call-done = bf16[224,7168]{1,0:T(8,128)(2,1)} async-done(((bf16[224,7168]{1,0:T(8,128)(2,1)}), bf16[224,7168]{1,0:T(8,128)(2,1)}) %all-reduce.2.cloned.1.call-update) | async-done | bytes 3211280 | tf_op jit(solution)/shard_map/psum | solution.py:47
  296.2 5.3 %fusion.3 = bf16[224,7168]{1,0:T(8,128)(2,1)S(1)} fusion(bf16[224,7168]{1,0:T(8,128)(2,1)} %all-reduce.2.cloned.1.call-done, bf16[1,224,7168]{2,1,0:T(8,128)(2,1)} %all-gather.16.cloned.1.call-done, bf16[1,224,7168]{2,1,0:T(8,128)(2,1)} %all-gather.18.cloned.1.call-done), kind=kLoop, calls=%fused_computation.13 | loop fusion | flops 20873216 | bytes 12845056 | tf_op jit(solution)/shard_map/convert_element_type | solution.py:13
  301.6 22.2 %all-gather.12.cloned.1.call-done = bf16[1024,7168]{1,0:T(8,128)(2,1)} async-done(((bf16[1024,3584]{1,0:T(8,128)(2,1)}), bf16[1024,7168]{1,0:T(8,128)(2,1)}) %all-gather.12.cloned.1.call-update) | async-done | bytes 14680080 | tf_op jit(solution)/shard_map/all_gather | solution.py:34
  323.8 8.7 %fusion.19 = f32[224,1024]{1,0:T(8,128)} fusion(bf16[224,7168]{1,0:T(8,128)(2,1)S(1)} %fusion.3, bf16[1024,7168]{1,0:T(8,128)(2,1)} %all-gather.12.cloned.1.call-done), kind=kOutput, calls=%fused_computation.27 | convolution fusion | flops 3288334336 | bytes 18808832 | tf_op jit(solution)/shard_map/dot_general | solution.py:21
  332.4 21.1 %all-gather.14.cloned.1.call-done = bf16[1024,7168]{1,0:T(8,128)(2,1)} async-done(((bf16[1024,3584]{1,0:T(8,128)(2,1)}), bf16[1024,7168]{1,0:T(8,128)(2,1)}) %all-gather.14.cloned.1.call-update) | async-done | bytes 14680080 | tf_op jit(solution)/shard_map/all_gather | solution.py:35
  353.5 12.8 %fusion.11 = bf16[224,1024]{1,0:T(8,128)(2,1)} fusion(f32[224,1024]{1,0:T(8,128)} %fusion.19, bf16[1024,7168]{1,0:T(8,128)(2,1)} %all-gather.14.cloned.1.call-done, bf16[224,7168]{1,0:T(8,128)(2,1)} %all-reduce.2.cloned.1.call-done, bf16[1,224,7168]{2,1,0:T(8,128)(2,1)} %all-gather.18.cloned.1.call-done), kind=kOutput, calls=%fused_computation.21 | convolution fusion | flops 3301638144 | bytes 22478848 | tf_op jit(solution)/shard_map/dot_general | solution.py:21
  366.3 0.0 reduce-scatter.2.cloned.1.call-update
  366.3 8.6 %convert_bitcast_fusion.2 = bf16[1,1024,7168]{1,2,0:T(8,128)(2,1)} fusion(bf16[224,7168]{1,0:T(8,128)(2,1)S(1)} %fusion.3, bf16[1,224,1024]{2,1,0:T(8,128)(2,1)} %all-gather.3), kind=kOutput, calls=%fused_computation.2 | convolution fusion | flops 3295674368 | bytes 18350080 | tf_op jit(solution)/shard_map/dot_general | solution.py:27
  374.9 0.0 copy-start
  374.9 20.1 %copy.11 = bf16[1,1024,7168]{2,1,0:T(8,128)(2,1)} copy(bf16[1,1024,7168]{1,2,0:T(8,128)(2,1)} %convert_bitcast_fusion.2) | data formatting | bytes 29360128
  395.0 0.0 copy-done
  395.0 11.7 %convert_bitcast_fusion.1 = bf16[1,1024,7168]{1,2,0:T(8,128)(2,1)} fusion(bf16[1,224,1024]{2,1,0:T(8,128)(2,1)} %all-gather.3, bf16[224,7168]{1,0:T(8,128)(2,1)} %all-reduce.2.cloned.1.call-done, bf16[1,224,7168]{2,1,0:T(8,128)(2,1)S(1)} %copy-done), kind=kOutput, calls=%fused_computation.1 | convolution fusion | flops 3308519424 | bytes 21561344 | tf_op jit(solution)/shard_map/dot_general | solution.py:27
  406.7 19.9 %copy.12 = bf16[1,1024,7168]{2,1,0:T(8,128)(2,1)} copy(bf16[1,1024,7168]{1,2,0:T(8,128)(2,1)} %convert_bitcast_fusion.1) | data formatting | bytes 29360128
  426.6 0.0 reduce-scatter.2.cloned.1.call-done
Async XLA Ops:
  7.2 2.3 copy-start.1
  7.2 32.2 %all-gather.10.cloned.1.call-start = ((), (), s32[]{:S(2)}) async-start(), calls=%async_computation.1 | async-start | bytes 22020096 | tf_op jit(solution)/shard_map/all_gather | solution.py:36
  7.9 98.8 %all-gather.18.cloned.1.call-start = ((), (), s32[]{:S(2)}) async-start(), calls=%async_computation.7 | async-start | bytes 4014080 | tf_op jit(solution)/shard_map/all_gather | solution.py:43
  8.7 162.9 %all-gather.16.cloned.1.call-start = ((), (), s32[]{:S(2)}) async-start(), calls=%async_computation.6 | async-start | bytes 4014080 | tf_op jit(solution)/shard_map/all_gather | solution.py:44
  9.4 286.8 %all-reduce.2.cloned.1.call-start = ((), (), s32[]{:S(2)}) async-start(), calls=%async_computation.2 | async-start | bytes 6422528 | tf_op jit(solution)/shard_map/psum | solution.py:47
  55.3 1.2 copy-start.2
  55.3 268.4 %all-gather.12.cloned.1.call-start = ((), (), s32[]{:S(2)}) async-start(), calls=%async_computation.3 | async-start | bytes 22020096 | tf_op jit(solution)/shard_map/all_gather | solution.py:34
  55.9 297.6 %all-gather.14.cloned.1.call-start = ((), (), s32[]{:S(2)}) async-start(), calls=%async_computation.4 | async-start | bytes 22020096 | tf_op jit(solution)/shard_map/all_gather | solution.py:35
  56.5 370.1 %reduce-scatter.2.cloned.1.call-start = ((), (), s32[]{:S(2)}) async-start(), calls=%async_computation.5 | async-start | bytes 688128 | tf_op jit(solution)/shard_map/reduce_scatter | solution.py:52
  374.9 20.1 %copy-start = (bf16[1,224,7168]{2,1,0:T(8,128)(2,1)S(1)}, bf16[1,224,7168]{2,1,0:T(8,128)(2,1)}, u32[]{:S(2)}) copy-start(bf16[1,224,7168]{2,1,0:T(8,128)(2,1)} %all-gather.18.cloned.1.call-done) | copy-start | bytes 9633796
Sparse Core Ops, SparseCore 0:
  9.6 29.7 all-gather.9
  40.9 65.7 all-gather.17
  108.3 63.2 all-gather.15
  174.3 121.8 all-reduce.1
  297.7 26.0 all-gather.11
  325.3 28.1 all-gather.13
  366.4 14.9 reduce-scatter.1
where the time goes:
time: 435 us; the launch traced here: 433 us
  waiting for transfers between devices  287 us (66%)
  matrix products  68.5 us (16%)
  local copies, waits for them, and re-layouts  40 us (9%)
  blocking collectives  17.9 us (4%)
  between operations  14.2 us (3%)
  other arithmetic  5.33 us (1%)
    psum x1, waiting for transfers between devices, shards(): lax.psum(partial_hidden.astype(jnp.bfloat16), 'col').astype(jnp.float32)  114 us
    all_gather x1, waiting for transfers between devices, shards(): lax.all_gather(up_pre[0], 'col', axis=0, tiled=True)  64.8 us
    all_gather x1, waiting for transfers between devices, shards(): lax.all_gather(gate_pre[0], 'col', axis=0, tiled=True)  41.4 us
    unnamed x8, local copies, waits for them, and re-layouts  40 us
    dot_general x3, matrix products, times_transposed(): lax.dot_general(left, right, (((1,), (1,)), ((), ())), preferred_element_...  37.4 us
    dot_general x3, matrix products, over_tokens(): lax.dot_general(left, right, (((0,), (0,)), ((), ())), preferred_element_...  31.2 us
    all_gather x1, waiting for transfers between devices, shards(): lax.all_gather(gate_weight, 'depth', axis=1, tiled=True)  22.2 us
    all_gather x1, waiting for transfers between devices, shards(): lax.all_gather(up_weight, 'depth', axis=1, tiled=True)  21.1 us
  transfers between devices with their start and end apart: 7, of which 6 were waited for; matrix products, arithmetic and copies ran while one was open for 23% of the time, Pallas kernels for 0%

commit v1 on v0

--- a/solution.py
+++ b/solution.py
@@ -44,7 +44,9 @@
         lax.all_gather(up_pre[0], "col", axis=0, tiled=True),
     )
     partial_hidden = times_transposed(grad_rows, down_full)
-    hidden_grad = lax.psum(partial_hidden.astype(jnp.bfloat16), "col").astype(jnp.float32)
+    hidden_grad = jnp.sum(
+        lax.all_gather(partial_hidden.astype(jnp.bfloat16), "col"), axis=0
+    ).astype(jnp.float32)
     gate_grad, up_grad, hidden = swiglu_grads(hidden_grad, gate_rows, up_rows)
     gate_wgrad = over_tokens(input_rows, gate_grad).astype(jnp.bfloat16)
     up_wgrad = over_tokens(input_rows, up_grad).astype(jnp.bfloat16)

time: 435 us -> 532 us (1.22)
  waiting for transfers between devices: 287 us -> 371 us
  other arithmetic: 5.33 us -> 17.5 us
    all_gather x0 -> x1, waiting for transfers between devices: none -> 211 us  [shards(): lax.all_gather(partial_hidden.astype(jnp.bfloat16), 'col')]
    psum x1 -> x0, waiting for transfers between devices: 114 us -> none  [shards(): lax.psum(partial_hidden.astype(jnp.bfloat16), 'col').astype(jnp.float32)]
    all_gather x1, waiting for transfers between devices: 22.2 us -> 9.16 us  [shards(): lax.all_gather(gate_weight, 'depth', axis=1, tiled=True)]
    reduce_sum x0 -> x1, other arithmetic: none -> 10.3 us  [shards(): jnp.sum(lax.all_gather(partial_hidden.astype(jnp.bfloat16), 'col'), axis=0)]
  transfers between devices with their start and end apart: 7 -> 7, of which waited for: 6 -> 6; matrix products, arithmetic and copies ran while one was open for 23% -> 22% of each run, Pallas kernels for 0% -> 0%
where the time goes in v1:
time: 532 us; the launch traced here: 531 us
  waiting for transfers between devices  371 us (70%)
  matrix products  69.6 us (13%)
  local copies, waits for them, and re-layouts  40 us (8%)
  blocking collectives  17.9 us (3%)
  other arithmetic  17.5 us (3%)
  between operations  14.2 us (3%)
    all_gather x1, waiting for transfers between devices, shards(): lax.all_gather(partial_hidden.astype(jnp.bfloat16), 'col')  211 us
    all_gather x1, waiting for transfers between devices, shards(): lax.all_gather(up_pre[0], 'col', axis=0, tiled=True)  64.8 us
    all_gather x1, waiting for transfers between devices, shards(): lax.all_gather(gate_pre[0], 'col', axis=0, tiled=True)  41.4 us
    unnamed x8, local copies, waits for them, and re-layouts  40 us
    dot_general x3, matrix products, times_transposed(): lax.dot_general(left, right, (((1,), (1,)), ((), ())), preferred_element_...  37.3 us
    dot_general x3, matrix products, over_tokens(): lax.dot_general(left, right, (((0,), (0,)), ((), ())), preferred_element_...  32.3 us
    all_gather x1, waiting for transfers between devices, shards(): lax.all_gather(up_weight, 'depth', axis=1, tiled=True)  21 us
    all_gather x1, waiting for transfers between devices, shards(): lax.all_gather(down_weight, 'depth', axis=0, tiled=True)  20.7 us
  transfers between devices with their start and end apart: 7, of which 6 were waited for; matrix products, arithmetic and copies ran while one was open for 22% of the time, Pallas kernels for 0%

profile of v1, /device:TPU:0, one launch (start us, length us, event | category | flops | bytes accessed | tf_op | source)
XLA Modules:
  0.0 530.9 jit_solution(2625344047398228511)
XLA Ops:
  7.2 0.0 copy-start.1
  7.2 0.0 all-gather.12.cloned.1.call-start
  7.2 0.7 all-gather.12.cloned.1.call-update
  7.9 0.0 all-gather.22.cloned.1.call-start
  8.0 0.7 all-gather.22.cloned.1.call-update
  8.7 0.0 all-gather.20.cloned.1.call-start
  8.7 0.7 all-gather.20.cloned.1.call-update
  9.4 0.0 all-gather.18.cloned.1.call-start
  9.4 0.0 copy-done.1
  9.4 9.2 %all-gather = bf16[1,224,1024]{2,1,0:T(8,128)(2,1)S(1)} all-gather(bf16[1,112,1024]{2,1,0:T(8,128)(2,1)S(1)} %copy-done.1), channel_id=2, replica_groups=mesh['groups'=2,'row'=2,'col'=4,'depth'=2] {'row'}, dimensions={1}, use_global_device_ids=true | all-gather | bytes 688128 | tf_op jit(solution)/shard_map/all_gather | solution.py:40
  18.7 20.7 %all-gather.12.cloned.1.call-done = bf16[7168,1024]{1,0:T(8,128)(2,1)} async-done(((bf16[3584,1024]{1,0:T(8,128)(2,1)}), bf16[7168,1024]{1,0:T(8,128)(2,1)}) %all-gather.12.cloned.1.call-update) | async-done | bytes 14680080 | tf_op jit(solution)/shard_map/all_gather | solution.py:36
  39.3 15.9 %convolution_convert_fusion = bf16[224,7168]{1,0:T(8,128)(2,1)} fusion(bf16[7168,1024]{1,0:T(8,128)(2,1)} %all-gather.12.cloned.1.call-done, bf16[1,224,1024]{2,1,0:T(8,128)(2,1)S(1)} %all-gather), kind=kOutput, calls=%fused_computation.6 | convolution fusion | flops 3289939968 | bytes 18350080 | tf_op jit(solution)/shard_map/dot_general | solution.py:21
  55.3 0.0 all-gather.18.cloned.1.call-update
  55.3 0.0 copy-start.2
  55.3 0.0 all-gather.14.cloned.1.call-start
  55.4 0.5 all-gather.14.cloned.1.call-update
  55.9 0.0 all-gather.16.cloned.1.call-start
  56.0 0.5 all-gather.16.cloned.1.call-update
  56.5 0.0 reduce-scatter.2.cloned.1.call-start
  56.5 0.0 copy-done.2
  56.5 8.7 %all-gather.4 = bf16[1,224,1024]{2,1,0:T(8,128)(2,1)} all-gather(bf16[1,112,1024]{2,1,0:T(8,128)(2,1)S(1)} %copy-done.2), channel_id=6, replica_groups=mesh['groups'=2,'row'=2,'col'=4,'depth'=2] {'row'}, dimensions={1}, use_global_device_ids=true | all-gather | bytes 688128 | tf_op jit(solution)/shard_map/all_gather | solution.py:39
  65.3 41.4 %all-gather.22.cloned.1.call-done = bf16[1,224,7168]{2,1,0:T(8,128)(2,1)} async-done(((bf16[1,56,7168]{2,1,0:T(8,128)(2,1)}), bf16[1,224,7168]{2,1,0:T(8,128)(2,1)}) %all-gather.22.cloned.1.call-update) | async-done | bytes 3211280 | tf_op jit(solution)/shard_map/all_gather | solution.py:43
  106.7 64.8 %all-gather.20.cloned.1.call-done = bf16[1,224,7168]{2,1,0:T(8,128)(2,1)} async-done(((bf16[1,56,7168]{2,1,0:T(8,128)(2,1)}), bf16[1,224,7168]{2,1,0:T(8,128)(2,1)}) %all-gather.20.cloned.1.call-update) | async-done | bytes 3211280 | tf_op jit(solution)/shard_map/all_gather | solution.py:44
  171.5 11.9 %convert_bitcast_fusion = bf16[1,7168,1024]{2,1,0:T(8,128)(2,1)} fusion(bf16[1,224,7168]{2,1,0:T(8,128)(2,1)} %all-gather.20.cloned.1.call-done, bf16[1,224,7168]{2,1,0:T(8,128)(2,1)} %all-gather.22.cloned.1.call-done, bf16[1,224,1024]{2,1,0:T(8,128)(2,1)S(1)} %all-gather), kind=kOutput, calls=%fused_computation | convolution fusion | flops 3308519424 | bytes 21561344 | tf_op jit(solution)/shard_map/dot_general | solution.py:27
  183.5 211.2 %all-gather.18.cloned.1.call-done = bf16[896,7168]{1,0:T(8,128)(2,1)} async-done(((bf16[224,7168]{1,0:T(8,128)(2,1)}), bf16[896,7168]{1,0:T(8,128)(2,1)}) %all-gather.18.cloned.1.call-update) | async-done | bytes 12845072 | tf_op jit(solution)/shard_map/all_gather | solution.py:48
  394.7 10.3 %reduce_sum.12 = bf16[224,7168]{1,0:T(8,128)(2,1)} reduce(bf16[4,224,7168]{2,1,0:T(8,128)(2,1)} %bitcast.45, bf16[]{:T(256)} %constant.1.clone.1), dimensions={0}, to_apply=%region_0.0 | reduce | flops 4816896 | bytes 16056322 | tf_op jit(solution)/shard_map/reduce_sum | solution.py:47
  405.0 7.2 %fusion.3 = bf16[224,7168]{1,0:T(8,128)(2,1)S(1)} fusion(bf16[224,7168]{1,0:T(8,128)(2,1)} %reduce_sum.12, bf16[1,224,7168]{2,1,0:T(8,128)(2,1)} %all-gather.20.cloned.1.call-done, bf16[1,224,7168]{2,1,0:T(8,128)(2,1)} %all-gather.22.cloned.1.call-done), kind=kLoop, calls=%fused_computation.13 | loop fusion | flops 20873216 | bytes 12845056 | tf_op jit(solution)/shard_map/convert_element_type | solution.py:13
  412.2 9.2 %all-gather.14.cloned.1.call-done = bf16[1024,7168]{1,0:T(8,128)(2,1)} async-done(((bf16[1024,3584]{1,0:T(8,128)(2,1)}), bf16[1024,7168]{1,0:T(8,128)(2,1)}) %all-gather.14.cloned.1.call-update) | async-done | bytes 14680080 | tf_op jit(solution)/shard_map/all_gather | solution.py:34
  421.3 8.7 %fusion.19 = f32[224,1024]{1,0:T(8,128)} fusion(bf16[224,7168]{1,0:T(8,128)(2,1)S(1)} %fusion.3, bf16[1024,7168]{1,0:T(8,128)(2,1)} %all-gather.14.cloned.1.call-done), kind=kOutput, calls=%fused_computation.27 | convolution fusion | flops 3288334336 | bytes 18808832 | tf_op jit(solution)/shard_map/dot_general | solution.py:21
  430.0 21.0 %all-gather.16.cloned.1.call-done = bf16[1024,7168]{1,0:T(8,128)(2,1)} async-done(((bf16[1024,3584]{1,0:T(8,128)(2,1)}), bf16[1024,7168]{1,0:T(8,128)(2,1)}) %all-gather.16.cloned.1.call-update) | async-done | bytes 14680080 | tf_op jit(solution)/shard_map/all_gather | solution.py:35
  451.0 12.7 %fusion.11 = bf16[224,1024]{1,0:T(8,128)(2,1)} fusion(f32[224,1024]{1,0:T(8,128)} %fusion.19, bf16[1024,7168]{1,0:T(8,128)(2,1)} %all-gather.16.cloned.1.call-done, bf16[224,7168]{1,0:T(8,128)(2,1)} %reduce_sum.12, bf16[1,224,7168]{2,1,0:T(8,128)(2,1)} %all-gather.22.cloned.1.call-done), kind=kOutput, calls=%fused_computation.21 | convolution fusion | flops 3301638144 | bytes 22478848 | tf_op jit(solution)/shard_map/dot_general | solution.py:21
  463.7 0.0 reduce-scatter.2.cloned.1.call-update
  463.7 8.6 %convert_bitcast_fusion.2 = bf16[1,1024,7168]{1,2,0:T(8,128)(2,1)} fusion(bf16[224,7168]{1,0:T(8,128)(2,1)S(1)} %fusion.3, bf16[1,224,1024]{2,1,0:T(8,128)(2,1)} %all-gather.4), kind=kOutput, calls=%fused_computation.2 | convolution fusion | flops 3295674368 | bytes 18350080 | tf_op jit(solution)/shard_map/dot_general | solution.py:27
  472.4 0.0 copy-start
  472.4 20.1 %copy.11 = bf16[1,1024,7168]{2,1,0:T(8,128)(2,1)} copy(bf16[1,1024,7168]{1,2,0:T(8,128)(2,1)} %convert_bitcast_fusion.2) | data formatting | bytes 29360128
  492.5 0.0 copy-done
  492.5 11.7 %convert_bitcast_fusion.1 = bf16[1,1024,7168]{1,2,0:T(8,128)(2,1)} fusion(bf16[1,224,1024]{2,1,0:T(8,128)(2,1)} %all-gather.4, bf16[224,7168]{1,0:T(8,128)(2,1)S(1)} %copy-done, bf16[1,224,7168]{2,1,0:T(8,128)(2,1)} %all-gather.22.cloned.1.call-done), kind=kOutput, calls=%fused_computation.1 | convolution fusion | flops 3308519424 | bytes 21561344 | tf_op jit(solution)/shard_map/dot_general | solution.py:27
  504.2 19.9 %copy.12 = bf16[1,1024,7168]{2,1,0:T(8,128)(2,1)} copy(bf16[1,1024,7168]{1,2,0:T(8,128)(2,1)} %convert_bitcast_fusion.1) | data formatting | bytes 29360128
  524.1 0.0 reduce-scatter.2.cloned.1.call-done
Async XLA Ops:
  7.2 2.3 copy-start.1
  7.2 32.2 %all-gather.12.cloned.1.call-start = ((), (), s32[]{:S(2)}) async-start(), calls=%async_computation.1 | async-start | bytes 22020096 | tf_op jit(solution)/shard_map/all_gather | solution.py:36
  7.9 98.8 %all-gather.22.cloned.1.call-start = ((), (), s32[]{:S(2)}) async-start(), calls=%async_computation.7 | async-start | bytes 4014080 | tf_op jit(solution)/shard_map/all_gather | solution.py:43
  8.7 162.9 %all-gather.20.cloned.1.call-start = ((), (), s32[]{:S(2)}) async-start(), calls=%async_computation.6 | async-start | bytes 4014080 | tf_op jit(solution)/shard_map/all_gather | solution.py:44
  9.4 385.3 %all-gather.18.cloned.1.call-start = ((), (), s32[]{:S(2)}) async-start(), calls=%async_computation.5 | async-start | bytes 16056320 | tf_op jit(solution)/shard_map/all_gather | solution.py:48
  55.3 1.2 copy-start.2
  55.3 366.0 %all-gather.14.cloned.1.call-start = ((), (), s32[]{:S(2)}) async-start(), calls=%async_computation.2 | async-start | bytes 22020096 | tf_op jit(solution)/shard_map/all_gather | solution.py:34
  55.9 395.1 %all-gather.16.cloned.1.call-start = ((), (), s32[]{:S(2)}) async-start(), calls=%async_computation.3 | async-start | bytes 22020096 | tf_op jit(solution)/shard_map/all_gather | solution.py:35
  56.5 467.6 %reduce-scatter.2.cloned.1.call-start = ((), (), s32[]{:S(2)}) async-start(), calls=%async_computation.4 | async-start | bytes 688128 | tf_op jit(solution)/shard_map/reduce_scatter | solution.py:54
  472.4 20.1 %copy-start = (bf16[224,7168]{1,0:T(8,128)(2,1)S(1)}, bf16[224,7168]{1,0:T(8,128)(2,1)}, u32[]{:S(2)}) copy-start(bf16[224,7168]{1,0:T(8,128)(2,1)} %reduce_sum.12) | copy-start | bytes 9633796
Sparse Core Ops, SparseCore 0:
  9.6 29.7 all-gather.11
  40.9 65.7 all-gather.21
  108.3 63.2 all-gather.19
  173.5 221.1 all-gather.17
  396.1 25.2 all-gather.13
  422.8 28.1 all-gather.15
  463.9 15.0 reduce-scatter.1
